TPU v7x, 512 devices: a whole 4x8x8 slice. The times are simulated.
512 devices in a mesh: lat: 16 (over x_hi, z), lon: 32 (over y, x_lo, core).
Axes of the slice: x: 4 (x_hi: 2, x_lo: 2; x = x_hi * 2 + x_lo), y: 8, z: 8, core: 2. Of those that a mesh axis runs over, the one named last changes fastest.
Arguments:
- fields: bfloat16 [192, 2, 512, 512], P('lat', None, 'lon'), may hold values from -6 to 6
- land_ids: int32 [192, 512], P('lat', 'lon'), may hold values from 0 to 2
- surface_table: bfloat16 [3, 512], replicated, may hold values from -6 to 6
- level_table: bfloat16 [2, 512], replicated, may hold values from -6 to 6
- norm_first: float32 [512], replicated, may hold values from 0.5 to 1.5
- qkv_first: bfloat16 [3, 512, 512], replicated, may hold values from -2 to 2
- out_first: bfloat16 [512, 512], P('lat'), may hold values from -0.25 to 0.25
- norm_merge2: float32 [2048], replicated, may hold values from 0.5 to 1.5
- merge_second: bfloat16 [2048, 1024], P('lat'), may hold values from -0.125 to 0.125
- norm_merge3: float32 [4096], replicated, may hold values from 0.5 to 1.5
- merge_third: bfloat16 [4096, 2048], P(None, 'lat'), may hold values from -0.09375 to 0.09375
- norm_third: float32 [2048], replicated, may hold values from 0.5 to 1.5
- qkv_third: bfloat16 [3, 2048, 1024], P(None, None, 'lat'), may hold values from -2 to 2
- out_third: bfloat16 [1024, 2048], P('lat'), may hold values from -0.1875 to 0.1875
- up_third: bfloat16 [2048, 1024], P('lat'), may hold values from -0.125 to 0.125
- up_second: bfloat16 [1024, 512], P('lat'), may hold values from -0.1875 to 0.1875
Outputs:
- decoded: bfloat16 [192, 2, 512, 512], P('lat', None, 'lon')
All inputs are finite; a program needn't handle non-finite values.
Results may differ from a plain program's by a relative error of at most 0.02.
Values may be sent and summed in bfloat16 or wider, within the bound.
No kernel may reach another device: no remote copies, remote signals or barrier semaphores. Data moves between devices by JAX's collectives and lax.ppermute only.
A program may use at most 64 MiB of HBM per device.

v0:
```python
import jax
import jax.numpy as jnp
from jax import lax
from jax.sharding import PartitionSpec as P

HD = 64


def with_halo(cells, sides, width):
    for axis, dim in sides:
        count = lax.axis_size(axis)
        head = lax.slice_in_dim(cells, 0, width, axis=dim)
        tail = lax.slice_in_dim(cells, cells.shape[dim] - width, cells.shape[dim], axis=dim)
        cells = jnp.concatenate(
            [
                lax.ppermute(tail, axis, [(i, (i + 1) % count) for i in range(count)]),
                cells,
                lax.ppermute(head, axis, [((i + 1) % count, i) for i in range(count)]),
            ],
            axis=dim,
        )
    return cells


def norm_rows(values, gain):
    row_mean = jnp.mean(values, axis=-1, keepdims=True)
    centred = values - row_mean
    spread = jnp.mean(centred * centred, axis=-1, keepdims=True)
    return centred * lax.rsqrt(spread + 1e-05) * gain


def split_quads(cell_grid):
    lat_count, levels, lon_count, feat_dim = cell_grid.shape
    blocks = cell_grid.reshape(lat_count // 2, 2, levels, lon_count // 2, 2, feat_dim)
    return blocks.transpose(0, 2, 3, 1, 4, 5).reshape(
        lat_count // 2, levels, lon_count // 2, 4 * feat_dim
    )


def spread_quads(cell_grid):
    lat_count, levels, lon_count, feat_dim = cell_grid.shape
    widened = jnp.broadcast_to(
        cell_grid[:, None, :, :, None, :], (lat_count, 2, levels, lon_count, 2, feat_dim)
    )
    return widened.reshape(2 * lat_count, levels, 2 * lon_count, feat_dim)


def to_windows(cell_grid):
    lat_count, levels, lon_count, feat_dim = cell_grid.shape
    blocks = cell_grid.reshape(lat_count // 4, 4, levels, lon_count // 4, 4, feat_dim).transpose(
        0, 3, 1, 2, 4, 5
    )
    return blocks.reshape(lat_count // 4 * (lon_count // 4), 16 * levels, feat_dim)


def from_windows(windows, lat_count, levels, lon_count):
    feat_dim = windows.shape[-1]
    blocks = windows.reshape(lat_count // 4, lon_count // 4, 4, levels, 4, feat_dim).transpose(
        0, 2, 3, 1, 4, 5
    )
    return blocks.reshape(lat_count, levels, lon_count, feat_dim)


def attend(query_in, key_in, value_in, head_count, key_mask):
    win_count, win_tokens, feat_dim = query_in.shape
    head_width = feat_dim // head_count
    query_heads = query_in.reshape(win_count, win_tokens, head_count, head_width)
    key_heads = key_in.reshape(win_count, win_tokens, head_count, head_width)
    value_heads = value_in.reshape(win_count, win_tokens, head_count, head_width)
    scores = jnp.einsum(
        "wqhd,wkhd->whqk", query_heads, key_heads, preferred_element_type=jnp.float32
    ) * head_width ** (-0.5)
    if key_mask is not None:
        scores = jnp.where(key_mask[:, None, None, :], scores, -1e30)
    row_peak = jnp.max(scores, axis=-1, keepdims=True)
    weights = jnp.exp(scores - row_peak)
    prob_bf = (weights / jnp.sum(weights, axis=-1, keepdims=True)).astype(jnp.bfloat16)
    mixed_out = jnp.einsum(
        "whqk,wkhd->wqhd", prob_bf, value_heads, preferred_element_type=jnp.float32
    )
    return mixed_out.astype(jnp.bfloat16).reshape(win_count, win_tokens, feat_dim)


def project_three(normed_rows, tables):
    return jnp.stack(
        [
            jnp.dot(normed_rows, tables[component], preferred_element_type=jnp.float32).astype(
                jnp.bfloat16
            )
            for component in range(3)
        ]
    )


def stream_rows(left_rows, shard):
    return jnp.dot(
        left_rows,
        lax.all_gather(shard, "lat", axis=0, tiled=True),
        preferred_element_type=jnp.float32,
    )


def on_device(
    fields,
    land_ids,
    surface_table,
    level_table,
    norm_first,
    qkv_first,
    out_first,
    norm_merge2,
    merge_second,
    norm_merge3,
    merge_third,
    norm_third,
    qkv_third,
    out_third,
    up_third,
    up_second,
):
    tile_rows, levels, tile_cols, feat_dim = fields.shape
    lat_count = lax.axis_size("lat")
    picks = (land_ids[:, :, None] == jnp.arange(3, dtype=jnp.int32)).astype(jnp.float32)
    surface = jnp.einsum("ijs,sc->ijc", picks, surface_table.astype(jnp.float32))
    hidden = (
        fields.astype(jnp.float32)
        + surface[:, None, :, :]
        + level_table.astype(jnp.float32)[None, :, None, :]
    ).astype(jnp.bfloat16)
    ext_rows = tile_rows + 4
    ext_cols = tile_cols + 4
    grown = with_halo(hidden, (("lat", 0), ("lon", 2)), 2)
    normed = (
        norm_rows(grown.astype(jnp.float32), norm_first).astype(jnp.bfloat16).reshape(-1, feat_dim)
    )
    triple = project_three(normed, qkv_first).reshape(3, ext_rows, levels, ext_cols, feat_dim)
    lat_place = lax.axis_index("lat") * tile_rows + jnp.arange(ext_rows) - 2
    valid_rows = (lat_place >= 0) & (lat_place < tile_rows * lat_count)
    mask_grid = jnp.broadcast_to(valid_rows[:, None, None, None], (ext_rows, levels, ext_cols, 1))
    key_mask = to_windows(mask_grid)[:, :, 0]
    window_parts = [to_windows(triple[component]) for component in range(3)]
    mixed_out = attend(window_parts[0], window_parts[1], window_parts[2], feat_dim // HD, key_mask)
    attended = from_windows(mixed_out, ext_rows, levels, ext_cols)[
        2 : tile_rows + 2, :, 2 : tile_cols + 2, :
    ]
    projected = stream_rows(attended.reshape(-1, feat_dim), out_first).reshape(hidden.shape)
    skip_first = (hidden.astype(jnp.float32) + projected).astype(jnp.bfloat16)
    quads = split_quads(skip_first)
    merged_in = norm_rows(quads.astype(jnp.float32), norm_merge2).astype(jnp.bfloat16)
    second_grid = stream_rows(merged_in.reshape(-1, quads.shape[-1]), merge_second).astype(
        jnp.bfloat16
    )
    second_grid = second_grid.reshape(tile_rows // 2, levels, tile_cols // 2, -1)
    quads_coarse = split_quads(second_grid)
    coarse_in = (
        norm_rows(quads_coarse.astype(jnp.float32), norm_merge3)
        .astype(jnp.bfloat16)
        .reshape(-1, quads_coarse.shape[-1])
    )
    own_count = coarse_in.shape[0]
    column_block = jnp.dot(
        lax.all_gather(coarse_in, "lat", axis=0, tiled=True),
        merge_third,
        preferred_element_type=jnp.float32,
    ).astype(jnp.bfloat16)
    coarse_full = lax.all_gather(column_block, "lat", axis=1, tiled=True)
    normed_coarse = norm_rows(coarse_full.astype(jnp.float32), norm_third).astype(jnp.bfloat16)
    head_feats = qkv_third.shape[2]
    coarse_rows = tile_rows // 4 * lat_count
    coarse_cols = tile_cols // 4
    triple_coarse = project_three(normed_coarse, qkv_third).reshape(
        3, coarse_rows, levels, coarse_cols, head_feats
    )
    coarse_parts = [to_windows(triple_coarse[component]) for component in range(3)]
    mixed_coarse = attend(coarse_parts[0], coarse_parts[1], coarse_parts[2], head_feats // HD, None)
    heads_out = from_windows(mixed_coarse, coarse_rows, levels, coarse_cols).reshape(-1, head_feats)
    own_coarse = lax.dynamic_slice_in_dim(
        coarse_full, lax.axis_index("lat") * own_count, own_count, 0
    )
    update = lax.psum_scatter(
        jnp.dot(heads_out, out_third, preferred_element_type=jnp.float32).astype(jnp.bfloat16),
        "lat",
        scatter_dimension=0,
        tiled=True,
    ).astype(jnp.float32)
    level_three = (own_coarse.astype(jnp.float32) + update).astype(jnp.bfloat16)
    lift_three = stream_rows(level_three, up_third).reshape(
        tile_rows // 4, levels, tile_cols // 4, -1
    )
    level_two = (second_grid.astype(jnp.float32) + spread_quads(lift_three)).astype(jnp.bfloat16)
    lift_two = stream_rows(level_two.reshape(-1, level_two.shape[-1]), up_second).reshape(
        tile_rows // 2, levels, tile_cols // 2, -1
    )
    return (skip_first.astype(jnp.float32) + spread_quads(lift_two)).astype(jnp.bfloat16)


def solution(mesh):
    in_specs = (
        P("lat", None, "lon", None),
        P("lat", "lon"),
        P(),
        P(),
        P(),
        P(),
        P("lat", None),
        P(),
        P("lat", None),
        P(),
        P(None, "lat"),
        P(),
        P(None, None, "lat"),
        P("lat", None),
        P("lat", None),
        P("lat", None),
    )
    out_specs = P("lat", None, "lon", None)
    return jax.shard_map(
        on_device, mesh=mesh, in_specs=in_specs, out_specs=out_specs, check_vma=False
    )
```

profile of v0, /device:TPU:1, one launch (start us, length us, event | category | flops | bytes accessed | tf_op | source)
XLA Modules:
  0.0 719.5 jit_solution(10384783542044688699)
XLA Ops:
  10.1 4.8 collective-permute-start
  14.9 11.0 %collective-permute-start.1 = (bf16[2,2,16,512]{3,2,1,0:T(8,128)(2,1)S(1)}, bf16[2,2,16,512]{3,2,1,0:T(8,128)(2,1)S(1)}, u32[]{:S(2)}, u32[]{:S(2)}) collective-permute-start(bf16[2,2,16,512]{3,2,1,0:T(8,128)(2,1)S(1)} %get-tuple-element.8), channel_id=1, source_target_pairs={{32,0},{64,32},{96,64},{128,96},{160,128},{192,160},{224,192},{256... | collective-permute-start | bytes 196616 | tf_op jit(solution)/shard_map/ppermute | solution.py:18
  26.0 37.2 %all_gather.18 = bf16[512,512]{1,0:T(8,128)(2,1)} all-gather(bf16[32,512]{1,0:T(8,128)(2,1)S(1)} %copy-done.7), channel_id=1, replica_groups=mesh['lat'=16,'lon'=32] {'lat'}, dimensions={0}, use_global_device_ids=true | all-gather | bytes 557056 | tf_op jit(solution)/shard_map/all_gather | solution.py:98
  63.3 9.8 %collective-permute-start.2 = (bf16[16,2,2,512]{3,2,1,0:T(2,128)(2,1)S(1)}, bf16[16,2,2,512]{3,2,1,0:T(2,128)(2,1)S(1)}, u32[]{:S(2)}, u32[]{:S(2)}) collective-permute-start(bf16[16,2,2,512]{3,2,1,0:T(2,128)(2,1)S(1)} %get-tuple-element.5), channel_id=1, source_target_pairs={{0,1},{1,2},{2,3},{3,4},{4,5},{5,6},{6,7},{7,8},{8,9},{9,10},{10,1... | collective-permute-start | bytes 196616 | tf_op jit(solution)/shard_map/ppermute | solution.py:16
  73.1 1.9 collective-permute-start.3
  75.3 5.1 collective-permute-done.3
  84.4 1.8 reshape_reshape.14
  88.2 1.7 reshape_reshape.15
  91.9 1.7 reshape_reshape.13
  93.6 4.6 fusion.63
  98.2 2.4 fusion.13
  106.2 13.9 %all-gather.6.cloned.1.call-done = bf16[2048,1024]{1,0:T(8,128)(2,1)} async-done(((bf16[128,1024]{1,0:T(8,128)(2,1)}), bf16[2048,1024]{1,0:T(8,128)(2,1)}) %all-gather.6.cloned.1.call-update) | async-done | bytes 4194320 | tf_op jit(solution)/shard_map/all_gather | solution.py:98
  120.1 3.0 fusion.25
  125.5 94.8 %all-gather.8.cloned.1.call-done = bf16[384,4096]{1,0:T(8,128)(2,1)} async-done(((bf16[24,4096]{1,0:T(8,128)(2,1)}), bf16[384,4096]{1,0:T(8,128)(2,1)}) %all-gather.8.cloned.1.call-update) | async-done | bytes 3145744 | tf_op jit(solution)/shard_map/all_gather | solution.py:162
  220.2 3.5 convolution_convert_fusion.6
  224.4 82.4 %all-gather.10.cloned.1.call-done = bf16[384,2048]{1,0:T(8,128)(2,1)} async-done(((bf16[384,128]{1,0:T(8,128)(2,1)}), bf16[384,2048]{1,0:T(8,128)(2,1)}) %all-gather.10.cloned.1.call-update) | async-done | bytes 1572880 | tf_op jit(solution)/shard_map/all_gather | solution.py:166
  306.8 1.8 convert_reduce_fusion
  309.8 1.5 convolution_convert_fusion.9
  311.5 1.5 convolution_convert_fusion.8
  317.9 1.7 convolution_convert_fusion
  320.2 92.0 %all-gather.12.cloned.1.call-done = bf16[2048,1024]{1,0:T(8,128)(2,1)} async-done(((bf16[128,1024]{1,0:T(8,128)(2,1)}), bf16[2048,1024]{1,0:T(8,128)(2,1)}) %all-gather.12.cloned.1.call-update) | async-done | bytes 4194320 | tf_op jit(solution)/shard_map/all_gather | solution.py:98
  412.3 209.7 %reduce-scatter.2.cloned.1.call-done = bf16[24,2048]{1,0:T(8,128)(2,1)} async-done(((bf16[384,2048]{1,0:T(8,128)(2,1)}), bf16[24,2048]{1,0:T(8,128)(2,1)}) %reduce-scatter.2.cloned.1.call-update) | async-done | bytes 98320 | tf_op jit(solution)/shard_map/reduce_scatter | solution.py:180
  622.0 3.0 fusion.46
  626.0 83.4 %all-gather.14.cloned.1.call-done = bf16[1024,512]{1,0:T(8,128)(2,1)} async-done(((bf16[64,512]{1,0:T(8,128)(2,1)}), bf16[1024,512]{1,0:T(8,128)(2,1)}) %all-gather.14.cloned.1.call-update) | async-done | bytes 1048592 | tf_op jit(solution)/shard_map/all_gather | solution.py:98
  (106 shorter events, 31.1 us)
Async XLA Ops:
  6.5 213.7 %copy-start = (bf16[4096,128]{1,0:T(8,128)(2,1)S(1)}, bf16[4096,128]{1,0:T(8,128)(2,1)}, u32[]{:S(2)}) copy-start(bf16[4096,128]{1,0:T(8,128)(2,1)} %param.26) | copy-start | bytes 3145732
  6.5 19.5 %copy-start.7 = (bf16[32,512]{1,0:T(8,128)(2,1)S(1)}, bf16[32,512]{1,0:T(8,128)(2,1)}, u32[]{:S(2)}) copy-start(bf16[32,512]{1,0:T(8,128)(2,1)} %param.22) | copy-start | bytes 98308
  6.5 113.6 %all-gather.6.cloned.1.call-start = ((), (), s32[]{:S(2)}) async-start(), calls=%async_computation.1 | async-start | bytes 4456448 | tf_op jit(solution)/shard_map/all_gather | solution.py:98
  7.3 213.0 %all-gather.8.cloned.1.call-start = ((), (), s32[]{:S(2)}) async-start(), calls=%async_computation.2 | async-start | bytes 3342336 | tf_op jit(solution)/shard_map/all_gather | solution.py:162
  10.1 71.5 %copy-start.11 = (f32[512]{0:T(512)S(1)}, f32[512]{0:T(512)}, u32[]{:S(2)}) copy-start(f32[512]{0:T(512)} %param.20) | copy-start | bytes 6148
  10.1 53.1 %collective-permute-start = (bf16[2,2,16,512]{3,2,1,0:T(8,128)(2,1)S(1)}, bf16[2,2,16,512]{3,2,1,0:T(8,128)(2,1)S(1)}, u32[]{:S(2)}, u32[]{:S(2)}) collective-permute-start(bf16[2,2,16,512]{3,2,1,0:T(8,128)(2,1)S(1)} %get-tuple-element.7), channel_id=1, source_target_pairs={{0,32},{32,64},{64,96},{96,128},{128,160},{160,192},{192,224},{224... | collective-permute-start | bytes 196616 | tf_op jit(solution)/shard_map/ppermute | solution.py:16
  14.9 48.3 %collective-permute-start.1 = (bf16[2,2,16,512]{3,2,1,0:T(8,128)(2,1)S(1)}, bf16[2,2,16,512]{3,2,1,0:T(8,128)(2,1)S(1)}, u32[]{:S(2)}, u32[]{:S(2)}) collective-permute-start(bf16[2,2,16,512]{3,2,1,0:T(8,128)(2,1)S(1)} %get-tuple-element.8), channel_id=1, source_target_pairs={{32,0},{64,32},{96,64},{128,96},{160,128},{192,160},{224,192},{256... | collective-permute-start | bytes 196616 | tf_op jit(solution)/shard_map/ppermute | solution.py:18
  63.3 12.0 %collective-permute-start.2 = (bf16[16,2,2,512]{3,2,1,0:T(2,128)(2,1)S(1)}, bf16[16,2,2,512]{3,2,1,0:T(2,128)(2,1)S(1)}, u32[]{:S(2)}, u32[]{:S(2)}) collective-permute-start(bf16[16,2,2,512]{3,2,1,0:T(2,128)(2,1)S(1)} %get-tuple-element.5), channel_id=1, source_target_pairs={{0,1},{1,2},{2,3},{3,4},{4,5},{5,6},{6,7},{7,8},{8,9},{9,10},{10,1... | collective-permute-start | bytes 196616 | tf_op jit(solution)/shard_map/ppermute | solution.py:16
  73.1 7.4 %collective-permute-start.3 = (bf16[16,2,2,512]{3,2,1,0:T(2,128)(2,1)S(1)}, bf16[16,2,2,512]{3,2,1,0:T(2,128)(2,1)S(1)}, u32[]{:S(2)}, u32[]{:S(2)}) collective-permute-start(bf16[16,2,2,512]{3,2,1,0:T(2,128)(2,1)S(1)} %get-tuple-element.6), channel_id=1, source_target_pairs={{1,0},{2,1},{3,2},{4,3},{5,4},{6,5},{7,6},{8,7},{9,8},{10,9},{11,1... | collective-permute-start | bytes 196616 | tf_op jit(solution)/shard_map/ppermute | solution.py:18
  93.6 4.6 copy-start.5
  101.9 1.0 copy-start.4
  104.1 16.0 %copy-start.9 = (f32[2048]{0:T(1024)S(1)}, f32[2048]{0:T(1024)}, u32[]{:S(2)}) copy-start(f32[2048]{0:T(1024)} %param.23) | copy-start | bytes 24580
  123.1 1.4 copy-start.2
  123.1 1.4 copy-start.8
  125.4 181.4 %all-gather.10.cloned.1.call-start = ((), (), s32[]{:S(2)}) async-start(), calls=%async_computation.3 | async-start | bytes 1671168 | tf_op jit(solution)/shard_map/all_gather | solution.py:166
  223.8 188.5 %all-gather.12.cloned.1.call-start = ((), (), s32[]{:S(2)}) async-start(), calls=%async_computation.5 | async-start | bytes 4456448 | tf_op jit(solution)/shard_map/all_gather | solution.py:98
  223.8 85.4 %copy-start.10 = (f32[2048]{0:T(1024)S(1)}, f32[2048]{0:T(1024)}, u32[]{:S(2)}) copy-start(f32[2048]{0:T(1024)} %param.27) | copy-start | bytes 24580
  224.3 397.6 %reduce-scatter.2.cloned.1.call-start = ((), (), s32[]{:S(2)}) async-start(), calls=%async_computation.4 | async-start | bytes 1671168 | tf_op jit(solution)/shard_map/reduce_scatter | solution.py:180
  306.8 1.9 copy-start.1
  315.3 2.6 copy-start.6
  319.7 389.8 %all-gather.14.cloned.1.call-start = ((), (), s32[]{:S(2)}) async-start(), calls=%async_computation.6 | async-start | bytes 1114112 | tf_op jit(solution)/shard_map/all_gather | solution.py:98
  624.9 1.0 copy-start.3
Sparse Core Ops, SparseCore 0:
  10.5 109.5 all-gather.5
  125.5 94.6 all-gather.7
  223.9 82.8 all-gather.9
  309.8 102.4 all-gather.11
  416.6 205.3 reduce-scatter.1
  625.5 83.9 all-gather.13
where the time goes:
time: 723 us; the launch traced here: 720 us
  waiting for transfers between devices  583 us (81%)
  blocking collectives  37.2 us (5%)
  matrix products  32.8 us (5%)
  starting transfers between devices  27.8 us (4%)
  local copies, waits for them, and re-layouts  14.8 us (2%)
  between operations  14 us (2%)
  other arithmetic  9.85 us (1%)
    reduce_scatter x1, waiting for transfers between devices, on_device(): lax.psum_scatter(jnp.dot(heads_out, out_third, preferred_element_type=jnp...  210 us
    all_gather x3, waiting for transfers between devices, stream_rows(): lax.all_gather(shard, 'lat', axis=0, tiled=True)  189 us
    all_gather x1, waiting for transfers between devices, on_device(): lax.all_gather(coarse_in, 'lat', axis=0, tiled=True)  94.8 us
    all_gather x1, waiting for transfers between devices, on_device(): coarse_full = lax.all_gather(column_block, 'lat', axis=1, tiled=True)  82.4 us
    all_gather x1, blocking collectives, stream_rows(): lax.all_gather(shard, 'lat', axis=0, tiled=True)  37.2 us
    ppermute x2, starting transfers between devices, with_halo(): lax.ppermute(tail, axis, [(i, (i + 1) % count) for i in range(count)])  14.6 us
  transfers between devices with their start and end apart: 10, of which 7 were waited for; matrix products, arithmetic and copies ran while one was open for 6% of the time, Pallas kernels for 0%

commit v1 on v0

--- a/solution.py
+++ b/solution.py
@@ -92,12 +92,74 @@
     )
 
 
-def stream_rows(left_rows, shard):
-    return jnp.dot(
-        left_rows,
-        lax.all_gather(shard, "lat", axis=0, tiled=True),
-        preferred_element_type=jnp.float32,
-    )
+Z_RING = 8
+RINGS = [[ring * Z_RING + place for place in range(Z_RING)] for ring in range(2)]
+
+
+def swap_cores(values):
+    count = lax.axis_size("lon")
+    return lax.ppermute(values, "lon", [(i, i ^ 1) for i in range(count)])
+
+
+def swap_rings(values):
+    count = lax.axis_size("lat")
+    return lax.ppermute(values, "lat", [(i, (i + Z_RING) % count) for i in range(count)])
+
+
+def swap_shards(values):
+    lon_count = lax.axis_size("lon")
+    pairs = []
+    for lat in range(lax.axis_size("lat")):
+        for lon in range(lon_count):
+            ring, place = divmod(lat, Z_RING)
+            target = (lat, lon)
+            if ring != lon % 2:
+                target = ((1 - ring) * Z_RING + place, lon ^ 1)
+            pairs.append((lat * lon_count + lon, target[0] * lon_count + target[1]))
+    return lax.ppermute(values, ("lat", "lon"), pairs)
+
+
+def ring_scatter(blocks):
+    return lax.all_to_all(blocks, "lat", 0, 0, axis_index_groups=RINGS, tiled=True)
+
+
+def ring_gather(values):
+    return ring_scatter(jnp.broadcast_to(values[None], (Z_RING,) + values.shape))
+
+
+def in_order(flag, own, other, axis):
+    return jnp.where(
+        flag == 0,
+        jnp.concatenate([own, other], axis=axis),
+        jnp.concatenate([other, own], axis=axis),
+    )
+
+
+def gather_weights(wide, narrow, ring, core):
+    wide_rows, columns = wide.shape[0], wide.shape[1] // 2
+    narrow_rows = narrow.shape[0] // 2
+    own = jnp.concatenate(
+        [
+            lax.dynamic_slice_in_dim(wide, core * columns, columns, 1),
+            lax.dynamic_slice_in_dim(narrow, core * narrow_rows, narrow_rows, 0),
+        ],
+        axis=0,
+    )[None]
+    both = in_order(ring, own, swap_rings(own), 0)
+    mine = lax.all_gather(both, "lat", axis=1, axis_index_groups=RINGS, tiled=True)
+    other = swap_cores(mine)
+    split = [
+        half.reshape(2, Z_RING, wide_rows + narrow_rows, columns) for half in (mine, other)
+    ]
+    wides = [half[:, :, :wide_rows].reshape(-1, columns) for half in split]
+    narrows = [half[:, :, None, wide_rows:] for half in split]
+    narrow_all = in_order(core, narrows[0], narrows[1], 2).reshape(-1, columns)
+    return wides, narrow_all
+
+
+def dot_halves(rows, halves, core):
+    parts = [jnp.dot(rows, half, preferred_element_type=jnp.float32) for half in halves]
+    return in_order(core, parts[0], parts[1], 1)
 
 
 def on_device(
@@ -120,6 +182,13 @@
 ):
     tile_rows, levels, tile_cols, feat_dim = fields.shape
     lat_count = lax.axis_size("lat")
+    ring = lax.axis_index("lat") // Z_RING
+    core = lax.axis_index("lon") % 2
+    merge_second_halves, out_first_all = gather_weights(merge_second, out_first, ring, core)
+    up_third_halves, up_second_all = gather_weights(up_third, up_second, ring, core)
+    merge_third = swap_shards(merge_third)
+    qkv_third = swap_shards(qkv_third)
+    out_third = swap_shards(out_third)
     picks = (land_ids[:, :, None] == jnp.arange(3, dtype=jnp.int32)).astype(jnp.float32)
     surface = jnp.einsum("ijs,sc->ijc", picks, surface_table.astype(jnp.float32))
     hidden = (
@@ -143,13 +212,15 @@
     attended = from_windows(mixed_out, ext_rows, levels, ext_cols)[
         2 : tile_rows + 2, :, 2 : tile_cols + 2, :
     ]
-    projected = stream_rows(attended.reshape(-1, feat_dim), out_first).reshape(hidden.shape)
+    projected = jnp.dot(
+        attended.reshape(-1, feat_dim), out_first_all, preferred_element_type=jnp.float32
+    ).reshape(hidden.shape)
     skip_first = (hidden.astype(jnp.float32) + projected).astype(jnp.bfloat16)
     quads = split_quads(skip_first)
     merged_in = norm_rows(quads.astype(jnp.float32), norm_merge2).astype(jnp.bfloat16)
-    second_grid = stream_rows(merged_in.reshape(-1, quads.shape[-1]), merge_second).astype(
-        jnp.bfloat16
-    )
+    second_grid = dot_halves(
+        merged_in.reshape(-1, quads.shape[-1]), merge_second_halves, core
+    ).astype(jnp.bfloat16)
     second_grid = second_grid.reshape(tile_rows // 2, levels, tile_cols // 2, -1)
     quads_coarse = split_quads(second_grid)
     coarse_in = (
@@ -158,39 +229,49 @@
         .reshape(-1, quads_coarse.shape[-1])
     )
     own_count = coarse_in.shape[0]
-    column_block = jnp.dot(
-        lax.all_gather(coarse_in, "lat", axis=0, tiled=True),
-        merge_third,
+    line = Z_RING * own_count
+
+    ring_tokens = ring_gather(coarse_in).reshape(line, -1)
+    column_block = jnp.stack(
+        [
+            jnp.dot(tokens, merge_third, preferred_element_type=jnp.float32).astype(jnp.bfloat16)
+            for tokens in (ring_tokens, swap_cores(ring_tokens))
+        ]
+    )
+    own_columns = ring_gather(column_block).transpose(1, 2, 0, 3).reshape(2, line, -1)
+    other_columns = swap_cores(own_columns)[::-1]
+    coarse_full = jnp.concatenate([own_columns, other_columns], axis=-1)
+    half = own_columns.shape[-1]
+    gain_third = in_order(core, norm_third[:half], norm_third[half:], 0)
+    qkv_rolled = in_order(core, qkv_third[:, :half], qkv_third[:, half:], 1)
+    normed_coarse = norm_rows(coarse_full.astype(jnp.float32), gain_third).astype(jnp.bfloat16)
+    head_feats = qkv_third.shape[2]
+    triple_coarse = project_three(normed_coarse.reshape(2 * line, -1), qkv_rolled)
+    coarse_parts = triple_coarse.reshape(3, -1, 16 * levels, head_feats)
+    heads_out = attend(
+        coarse_parts[0], coarse_parts[1], coarse_parts[2], head_feats // HD, None
+    ).reshape(2, line, head_feats)
+    head_part = jnp.dot(heads_out, out_third, preferred_element_type=jnp.float32)
+    chip_part = head_part[0] + swap_cores(head_part[1].astype(jnp.bfloat16)).astype(jnp.float32)
+    update = jnp.sum(
+        ring_scatter(chip_part.astype(jnp.bfloat16).reshape(Z_RING, own_count, -1)).astype(
+            jnp.float32
+        ),
+        axis=0,
+    )
+    place = lax.axis_index("lat") % Z_RING
+    own_coarse = lax.dynamic_slice_in_dim(coarse_full[0], place * own_count, own_count, 0)
+    own_coarse = in_order(core, own_coarse[:, :half], own_coarse[:, half:], 1)
+    level_three = (own_coarse.astype(jnp.float32) + update).astype(jnp.bfloat16)
+    lift_three = dot_halves(level_three, up_third_halves, core).reshape(
+        tile_rows // 4, levels, tile_cols // 4, -1
+    )
+    level_two = (second_grid.astype(jnp.float32) + spread_quads(lift_three)).astype(jnp.bfloat16)
+    lift_two = jnp.dot(
+        level_two.reshape(-1, level_two.shape[-1]),
+        up_second_all,
         preferred_element_type=jnp.float32,
-    ).astype(jnp.bfloat16)
-    coarse_full = lax.all_gather(column_block, "lat", axis=1, tiled=True)
-    normed_coarse = norm_rows(coarse_full.astype(jnp.float32), norm_third).astype(jnp.bfloat16)
-    head_feats = qkv_third.shape[2]
-    coarse_rows = tile_rows // 4 * lat_count
-    coarse_cols = tile_cols // 4
-    triple_coarse = project_three(normed_coarse, qkv_third).reshape(
-        3, coarse_rows, levels, coarse_cols, head_feats
-    )
-    coarse_parts = [to_windows(triple_coarse[component]) for component in range(3)]
-    mixed_coarse = attend(coarse_parts[0], coarse_parts[1], coarse_parts[2], head_feats // HD, None)
-    heads_out = from_windows(mixed_coarse, coarse_rows, levels, coarse_cols).reshape(-1, head_feats)
-    own_coarse = lax.dynamic_slice_in_dim(
-        coarse_full, lax.axis_index("lat") * own_count, own_count, 0
-    )
-    update = lax.psum_scatter(
-        jnp.dot(heads_out, out_third, preferred_element_type=jnp.float32).astype(jnp.bfloat16),
-        "lat",
-        scatter_dimension=0,
-        tiled=True,
-    ).astype(jnp.float32)
-    level_three = (own_coarse.astype(jnp.float32) + update).astype(jnp.bfloat16)
-    lift_three = stream_rows(level_three, up_third).reshape(
-        tile_rows // 4, levels, tile_cols // 4, -1
-    )
-    level_two = (second_grid.astype(jnp.float32) + spread_quads(lift_three)).astype(jnp.bfloat16)
-    lift_two = stream_rows(level_two.reshape(-1, level_two.shape[-1]), up_second).reshape(
-        tile_rows // 2, levels, tile_cols // 2, -1
-    )
+    ).reshape(tile_rows // 2, levels, tile_cols // 2, -1)
     return (skip_first.astype(jnp.float32) + spread_quads(lift_two)).astype(jnp.bfloat16)
 
 

time: 723 us -> 267 us (0.37)
  waiting for transfers between devices: 583 us -> 99.4 us
  starting transfers between devices: 27.8 us -> 72.1 us
  blocking collectives: 37.2 us -> 0 us
  local copies, waits for them, and re-layouts: 14.8 us -> 39.7 us
  matrix products: 32.8 us -> 24.1 us
    all_gather x5 -> x2, waiting for transfers between devices: 367 us -> 17.4 us  [gather_weights(): lax.all_gather(both, 'lat', axis=1, axis_index_groups=RINGS, tiled=True)]
    reduce_scatter x1 -> x0, waiting for transfers between devices: 210 us -> none  [on_device(): lax.psum_scatter(jnp.dot(heads_out, out_third, preferred_element_type=jnp...]
    all_to_all x0 -> x3, waiting for transfers between devices: none -> 54.4 us  [ring_scatter(): lax.all_to_all(blocks, 'lat', 0, 0, axis_index_groups=RINGS, tiled=True)]
    ppermute x0 -> x10, starting transfers between devices: none -> 37.7 us  [the longest x5 15.7 us: swap_cores(): return lax.ppermute(values, 'lon', [(i, i ^ 1) for i in range(count)])]
    all_gather x1 -> x0, blocking collectives: 37.2 us -> none  [stream_rows(): lax.all_gather(shard, 'lat', axis=0, tiled=True)]
    ppermute x0 -> x10, waiting for transfers between devices: none -> 22.4 us  [the longest x3 13.4 us: swap_shards(): return lax.ppermute(values, ('lat', 'lon'), pairs)]
    slice x0 -> x9, local copies, waits for them, and re-layouts: none -> 12.7 us  [the longest x4 12.5 us: gather_weights(): wides = [half[:, :, :wide_rows].reshape(-1, columns) for half in split]]
    all_to_all x0 -> x3, starting transfers between devices: none -> 11.8 us  [ring_scatter(): lax.all_to_all(blocks, 'lat', 0, 0, axis_index_groups=RINGS, tiled=True)]
  transfers between devices with their start and end apart: 10 -> 19, of which waited for: 7 -> 10; matrix products, arithmetic and copies ran while one was open for 6% -> 20% of each run, Pallas kernels for 0% -> 0%
where the time goes in v1:
time: 267 us; the launch traced here: 263 us
  waiting for transfers between devices  99.4 us (37%)
  starting transfers between devices  72.1 us (27%)
  local copies, waits for them, and re-layouts  39.7 us (15%)
  matrix products  24.1 us (9%)
  between operations  14.4 us (5%)
  other arithmetic  13.4 us (5%)
    all_to_all x3, waiting for transfers between devices, ring_scatter(): lax.all_to_all(blocks, 'lat', 0, 0, axis_index_groups=RINGS, tiled=True)  54.4 us
    all_gather x2, waiting for transfers between devices, gather_weights(): lax.all_gather(both, 'lat', axis=1, axis_index_groups=RINGS, tiled=True)  17.4 us
    ppermute x5, starting transfers between devices, swap_cores(): return lax.ppermute(values, 'lon', [(i, i ^ 1) for i in range(count)])  15.7 us
    ppermute x3, waiting for transfers between devices, swap_shards(): return lax.ppermute(values, ('lat', 'lon'), pairs)  13.4 us
    ppermute x2, starting transfers between devices, with_halo(): lax.ppermute(head, axis, [((i + 1) % count, i) for i in range(count)])  13.1 us
    slice x4, local copies, waits for them, and re-layouts, gather_weights(): wides = [half[:, :, :wide_rows].reshape(-1, columns) for half in split]  12.5 us
    ppermute x3, starting transfers between devices, swap_shards(): return lax.ppermute(values, ('lat', 'lon'), pairs)  11.8 us
    all_to_all x3, starting transfers between devices, ring_scatter(): lax.all_to_all(blocks, 'lat', 0, 0, axis_index_groups=RINGS, tiled=True)  11.8 us
  transfers between devices with their start and end apart: 19, of which 10 were waited for; matrix products, arithmetic and copies ran while one was open for 20% of the time, Pallas kernels for 0%

profile of v1, /device:TPU:1, one launch (start us, length us, event | category | flops | bytes accessed | tf_op | source)
XLA Modules:
  0.0 263.1 jit_solution(3061183399597555485)
XLA Ops:
  8.2 5.5 %collective-permute-start.4 = (bf16[1,144,512]{2,1,0:T(8,128)(2,1)S(1)}, bf16[1,144,512]{2,1,0:T(8,128)(2,1)S(1)}, u32[]{:S(2)}, u32[]{:S(2)}) collective-permute-start(bf16[1,144,512]{2,1,0:T(8,128)(2,1)S(1)} %maximum_bitcast_fusion.1), channel_id=1, source_target_pairs={{0,256},{32,288},{64,320},{96,352},{128,384},{160,416},{192,448},{... | collective-permute-start | bytes 442376 | tf_op jit(solution)/shard_map/ppermute | solution.py:106
  18.8 4.9 %collective-permute-start = (bf16[2,2,16,512]{3,2,1,0:T(8,128)(2,1)S(1)}, bf16[2,2,16,512]{3,2,1,0:T(8,128)(2,1)S(1)}, u32[]{:S(2)}, u32[]{:S(2)}) collective-permute-start(bf16[2,2,16,512]{3,2,1,0:T(8,128)(2,1)S(1)} %get-tuple-element.11), channel_id=1, source_target_pairs={{0,32},{32,64},{64,96},{96,128},{128,160},{160,192},{192,224},{224... | collective-permute-start | bytes 196616 | tf_op jit(solution)/shard_map/ppermute | solution.py:16
  23.8 11.0 %collective-permute-start.1 = (bf16[2,2,16,512]{3,2,1,0:T(8,128)(2,1)S(1)}, bf16[2,2,16,512]{3,2,1,0:T(8,128)(2,1)S(1)}, u32[]{:S(2)}, u32[]{:S(2)}) collective-permute-start(bf16[2,2,16,512]{3,2,1,0:T(8,128)(2,1)S(1)} %get-tuple-element.12), channel_id=1, source_target_pairs={{32,0},{64,32},{96,64},{128,96},{160,128},{192,160},{224,192},{256... | collective-permute-start | bytes 196616 | tf_op jit(solution)/shard_map/ppermute | solution.py:18
  36.2 4.5 %collective-permute-start.2 = (bf16[16,2,2,512]{3,2,1,0:T(2,128)(2,1)S(1)}, bf16[16,2,2,512]{3,2,1,0:T(2,128)(2,1)S(1)}, u32[]{:S(2)}, u32[]{:S(2)}) collective-permute-start(bf16[16,2,2,512]{3,2,1,0:T(2,128)(2,1)S(1)} %get-tuple-element.9), channel_id=1, source_target_pairs={{0,1},{1,2},{2,3},{3,4},{4,5},{5,6},{6,7},{7,8},{8,9},{9,10},{10,1... | collective-permute-start | bytes 196616 | tf_op jit(solution)/shard_map/ppermute | solution.py:16
  43.1 3.9 %collective-permute-done.3 = bf16[16,2,2,512]{3,2,1,0:T(2,128)(2,1)S(1)} collective-permute-done((bf16[16,2,2,512]{3,2,1,0:T(2,128)(2,1)S(1)}, bf16[16,2,2,512]{3,2,1,0:T(2,128)(2,1)S(1)}, u32[]{:S(2)}, u32[]{:S(2)}) %collective-permute-start.3) | collective-permute-done | bytes 65568 | tf_op jit(solution)/shard_map/ppermute | solution.py:18
  48.2 17.4 %all-gather.3.cloned.1.call-done = bf16[2,1152,512]{2,1,0:T(8,128)(2,1)} async-done(((bf16[2,144,512]{2,1,0:T(8,128)(2,1)}), bf16[2,1152,512]{2,1,0:T(8,128)(2,1)}) %all-gather.3.cloned.1.call-update) | async-done | bytes 2359312 | tf_op jit(solution)/shard_map/all_gather | solution.py:149
  65.5 5.7 %collective-permute-start.5 = (bf16[2,1152,512]{2,1,0:T(8,128)(2,1)}, bf16[2,1152,512]{2,1,0:T(8,128)(2,1)}, u32[]{:S(2)}, u32[]{:S(2)}) collective-permute-start(bf16[2,1152,512]{2,1,0:T(8,128)(2,1)} %all-gather.3.cloned.1.call-done), channel_id=1, source_target_pairs={{0,1},{1,0},{2,3},{3,2},{4,5},{5,4},{6,7},{7,6},{8,9},{9,8},{10,11... | collective-permute-start | bytes 7077896 | tf_op jit(solution)/shard_map/ppermute | solution.py:101
  83.0 4.1 %fusion.63 = (f32[20,8,32]{2,1,0:T(8,128)S(1)}, f32[20,8,32,32]{2,3,1,0:T(8,128)}) fusion(pred[20,32]{1,0:T(8,128)(4,1)S(1)} %copy.74, bf16[20,32,8,64]{3,2,1,0:T(8,128)(2,1)} %reshape_reshape.18, bf16[20,32,8,64]{3,2,1,0:T(8,128)(2,1)S(1)} %reshape_reshape.17), kind=kOutput, calls=%fused_computation.143 | convolution fusion | flops 21626912 | bytes 1987200 | tf_op jit(solution)/shard_map/sub | solution.py:76
  92.1 3.1 %slice.133 = bf16[2,8,128,512]{3,2,1,0:T(8,128)(2,1)} slice(bf16[2,8,144,512]{3,2,1,0:T(8,128)(2,1)} %bitcast.178), slice={[0:2], [0:8], [0:128], [0:512]} | slice | bytes 4194304 | tf_op jit(solution)/shard_map/slice | solution.py:154
  97.2 3.1 %slice.134 = bf16[2,8,128,512]{3,2,1,0:T(8,128)(2,1)} slice(bf16[2,8,144,512]{3,2,1,0:T(8,128)(2,1)} %bitcast.13), slice={[0:2], [0:8], [0:128], [0:512]} | slice | bytes 4194304 | tf_op jit(solution)/shard_map/slice | solution.py:154
  109.2 4.5 %all-to-all-start = ((bf16[8,24,4096]{2,1,0:T(8,128)(2,1)}), bf16[8,24,4096]{2,1,0:T(8,128)(2,1)S(1)}, u32[]{:S(2)}, u32[]{:S(2)}) async-start(bf16[8,24,4096]{2,1,0:T(8,128)(2,1)} %broadcast_in_dim.37), calls=%async_computation | async-start | bytes 3145728 | tf_op jit(solution)/shard_map/all_to_all | solution.py:123
  113.8 4.7 %collective-permute-start.12 = (bf16[1,160,512]{2,1,0:T(8,128)(2,1)S(1)}, bf16[1,160,512]{2,1,0:T(8,128)(2,1)S(1)}, u32[]{:S(2)}, u32[]{:S(2)}) collective-permute-start(bf16[1,160,512]{2,1,0:T(8,128)(2,1)S(1)} %maximum_bitcast_fusion), channel_id=1, source_target_pairs={{0,256},{32,288},{64,320},{96,352},{128,384},{160,416},{192,448},{... | collective-permute-start | bytes 491528 | tf_op jit(solution)/shard_map/ppermute | solution.py:106
  118.5 4.2 %collective-permute-done.12 = bf16[1,160,512]{2,1,0:T(8,128)(2,1)S(1)} collective-permute-done((bf16[1,160,512]{2,1,0:T(8,128)(2,1)S(1)}, bf16[1,160,512]{2,1,0:T(8,128)(2,1)S(1)}, u32[]{:S(2)}, u32[]{:S(2)}) %collective-permute-start.12) | collective-permute-done | bytes 163872 | tf_op jit(solution)/shard_map/ppermute | solution.py:106
  123.5 34.9 %all-to-all-done = bf16[8,24,4096]{2,1,0:T(8,128)(2,1)S(1)} async-done(((bf16[8,24,4096]{2,1,0:T(8,128)(2,1)}), bf16[8,24,4096]{2,1,0:T(8,128)(2,1)S(1)}, u32[]{:S(2)}, u32[]{:S(2)}) %all-to-all-start) | async-done | bytes 1572896 | tf_op jit(solution)/shard_map/all_to_all | solution.py:123
  161.0 4.7 %collective-permute-start.6 = (bf16[4096,128]{1,0:T(8,128)(2,1)}, bf16[4096,128]{1,0:T(8,128)(2,1)S(1)}, u32[]{:S(2)}, u32[]{:S(2)}) collective-permute-start(bf16[4096,128]{1,0:T(8,128)(2,1)} %param.26), channel_id=1, source_target_pairs={{0,0},{1,256},{2,2},{3,258},{4,4},{5,260},{6,6},{7,262},{8,8},{9,2... | collective-permute-start | bytes 3145736 | tf_op jit(solution)/shard_map/ppermute | solution.py:119
  165.7 13.4 %collective-permute-done.6 = bf16[4096,128]{1,0:T(8,128)(2,1)S(1)} collective-permute-done((bf16[4096,128]{1,0:T(8,128)(2,1)}, bf16[4096,128]{1,0:T(8,128)(2,1)S(1)}, u32[]{:S(2)}, u32[]{:S(2)}) %collective-permute-start.6) | collective-permute-done | bytes 1048608 | tf_op jit(solution)/shard_map/ppermute | solution.py:119
  181.3 3.5 %all-to-all-start.1 = ((bf16[8,2,192,128]{3,2,1,0:T(8,128)(2,1)}), bf16[8,2,192,128]{3,2,1,0:T(8,128)(2,1)S(1)}, u32[]{:S(2)}, u32[]{:S(2)}) async-start(bf16[8,2,192,128]{3,2,1,0:T(8,128)(2,1)} %broadcast_in_dim.38), calls=%async_computation.1 | async-start | bytes 1572864 | tf_op jit(solution)/shard_map/all_to_all | solution.py:123
  184.8 4.5 %collective-permute-start.9 = (bf16[3,2048,64]{1,2,0:T(8,128)(2,1)}, bf16[3,2048,64]{1,2,0:T(8,128)(2,1)S(1)}, u32[]{:S(2)}, u32[]{:S(2)}) collective-permute-start(bf16[3,2048,64]{1,2,0:T(8,128)(2,1)} %param.28), channel_id=1, source_target_pairs={{0,0},{1,256},{2,2},{3,258},{4,4},{5,260},{6,6},{7,262},{8,8},{9,2... | collective-permute-start | bytes 2359304 | tf_op jit(solution)/shard_map/ppermute | solution.py:119
  192.0 7.8 %all-to-all-done.1 = bf16[8,2,192,128]{3,2,1,0:T(8,128)(2,1)S(1)} async-done(((bf16[8,2,192,128]{3,2,1,0:T(8,128)(2,1)}), bf16[8,2,192,128]{3,2,1,0:T(8,128)(2,1)S(1)}, u32[]{:S(2)}, u32[]{:S(2)}) %all-to-all-start.1) | async-done | bytes 786464 | tf_op jit(solution)/shard_map/all_to_all | solution.py:123
  203.0 3.5 %collective-permute-start.13 = (bf16[2,1280,512]{2,1,0:T(8,128)(2,1)}, bf16[2,1280,512]{2,1,0:T(8,128)(2,1)}, u32[]{:S(2)}, u32[]{:S(2)}) collective-permute-start(bf16[2,1280,512]{2,1,0:T(8,128)(2,1)} %all-gather.5.cloned.1.call-done), channel_id=1, source_target_pairs={{0,1},{1,0},{2,3},{3,2},{4,5},{5,4},{6,7},{7,6},{8,9},{9,8},{10,11... | collective-permute-start | bytes 7864328 | tf_op jit(solution)/shard_map/ppermute | solution.py:101
  225.2 3.8 %all-to-all-start.2 = ((bf16[8,24,2048]{2,1,0:T(8,128)(2,1)}), bf16[8,24,2048]{2,1,0:T(8,128)(2,1)S(1)}, u32[]{:S(2)}, u32[]{:S(2)}) async-start(bf16[8,24,2048]{2,1,0:T(8,128)(2,1)} %bitcast.170), calls=%async_computation.2 | async-start | bytes 1572864 | tf_op jit(solution)/shard_map/all_to_all | solution.py:123
  230.1 3.1 %slice.146 = bf16[2,8,128,512]{3,2,1,0:T(8,128)(2,1)} slice(bf16[2,8,160,512]{3,2,1,0:T(8,128)(2,1)} %bitcast.173), slice={[0:2], [0:8], [0:128], [0:512]} | slice | bytes 4194304 | tf_op jit(solution)/shard_map/slice | solution.py:154
  233.3 3.1 %slice.147 = bf16[2,8,128,512]{3,2,1,0:T(8,128)(2,1)} slice(bf16[2,8,160,512]{3,2,1,0:T(8,128)(2,1)} %bitcast.50), slice={[0:2], [0:8], [0:128], [0:512]} | slice | bytes 4194304 | tf_op jit(solution)/shard_map/slice | solution.py:154
  238.9 11.7 %all-to-all-done.2 = bf16[8,24,2048]{2,1,0:T(8,128)(2,1)S(1)} async-done(((bf16[8,24,2048]{2,1,0:T(8,128)(2,1)}), bf16[8,24,2048]{2,1,0:T(8,128)(2,1)S(1)}, u32[]{:S(2)}, u32[]{:S(2)}) %all-to-all-start.2) | async-done | bytes 786464 | tf_op jit(solution)/shard_map/all_to_all | solution.py:123
  (172 shorter events, 77.9 us)
Async XLA Ops:
  6.5 12.1 %copy-start.10 = (bf16[12,2,16,512]{3,2,1,0:T(8,128)(2,1)S(1)}, bf16[12,2,16,512]{3,2,1,0:T(8,128)(2,1)}, u32[]{:S(2)}) copy-start(bf16[12,2,16,512]{3,2,1,0:T(8,128)(2,1)} %param.16) | copy-start | bytes 1179652
  6.5 59.0 %all-gather.3.cloned.1.call-start = ((), (), s32[]{:S(2)}) async-start(), calls=%async_computation.3 | async-start | bytes 2654208 | tf_op jit(solution)/shard_map/all_gather | solution.py:149
  8.2 8.0 %collective-permute-start.4 = (bf16[1,144,512]{2,1,0:T(8,128)(2,1)S(1)}, bf16[1,144,512]{2,1,0:T(8,128)(2,1)S(1)}, u32[]{:S(2)}, u32[]{:S(2)}) collective-permute-start(bf16[1,144,512]{2,1,0:T(8,128)(2,1)S(1)} %maximum_bitcast_fusion.1), channel_id=1, source_target_pairs={{0,256},{32,288},{64,320},{96,352},{128,384},{160,416},{192,448},{... | collective-permute-start | bytes 442376 | tf_op jit(solution)/shard_map/ppermute | solution.py:106
  17.0 26.1 %copy-start.15 = (f32[2048]{0:T(1024)S(1)}, f32[2048]{0:T(1024)}, u32[]{:S(2)}) copy-start(f32[2048]{0:T(1024)} %param.23) | copy-start | bytes 24580
  18.7 52.6 %copy-start.16 = (f32[512]{0:T(512)S(1)}, f32[512]{0:T(512)}, u32[]{:S(2)}) copy-start(f32[512]{0:T(512)} %param.20) | copy-start | bytes 6148
  18.8 16.0 %collective-permute-start = (bf16[2,2,16,512]{3,2,1,0:T(8,128)(2,1)S(1)}, bf16[2,2,16,512]{3,2,1,0:T(8,128)(2,1)S(1)}, u32[]{:S(2)}, u32[]{:S(2)}) collective-permute-start(bf16[2,2,16,512]{3,2,1,0:T(8,128)(2,1)S(1)} %get-tuple-element.11), channel_id=1, source_target_pairs={{0,32},{32,64},{64,96},{96,128},{128,160},{160,192},{192,224},{224... | collective-permute-start | bytes 196616 | tf_op jit(solution)/shard_map/ppermute | solution.py:16
  23.8 12.4 %collective-permute-start.1 = (bf16[2,2,16,512]{3,2,1,0:T(8,128)(2,1)S(1)}, bf16[2,2,16,512]{3,2,1,0:T(8,128)(2,1)S(1)}, u32[]{:S(2)}, u32[]{:S(2)}) collective-permute-start(bf16[2,2,16,512]{3,2,1,0:T(8,128)(2,1)S(1)} %get-tuple-element.12), channel_id=1, source_target_pairs={{32,0},{64,32},{96,64},{128,96},{160,128},{192,160},{224,192},{256... | collective-permute-start | bytes 196616 | tf_op jit(solution)/shard_map/ppermute | solution.py:18
  36.2 6.9 %collective-permute-start.2 = (bf16[16,2,2,512]{3,2,1,0:T(2,128)(2,1)S(1)}, bf16[16,2,2,512]{3,2,1,0:T(2,128)(2,1)S(1)}, u32[]{:S(2)}, u32[]{:S(2)}) collective-permute-start(bf16[16,2,2,512]{3,2,1,0:T(2,128)(2,1)S(1)} %get-tuple-element.9), channel_id=1, source_target_pairs={{0,1},{1,2},{2,3},{3,4},{4,5},{5,6},{6,7},{7,8},{8,9},{9,10},{10,1... | collective-permute-start | bytes 196616 | tf_op jit(solution)/shard_map/ppermute | solution.py:16
  40.8 6.3 %collective-permute-start.3 = (bf16[16,2,2,512]{3,2,1,0:T(2,128)(2,1)S(1)}, bf16[16,2,2,512]{3,2,1,0:T(2,128)(2,1)S(1)}, u32[]{:S(2)}, u32[]{:S(2)}) collective-permute-start(bf16[16,2,2,512]{3,2,1,0:T(2,128)(2,1)S(1)} %get-tuple-element.10), channel_id=1, source_target_pairs={{1,0},{2,1},{3,2},{4,3},{5,4},{6,5},{7,6},{8,7},{9,8},{10,9},{11,1... | collective-permute-start | bytes 196616 | tf_op jit(solution)/shard_map/ppermute | solution.py:18
  65.5 30.7 %collective-permute-start.5 = (bf16[2,1152,512]{2,1,0:T(8,128)(2,1)}, bf16[2,1152,512]{2,1,0:T(8,128)(2,1)}, u32[]{:S(2)}, u32[]{:S(2)}) collective-permute-start(bf16[2,1152,512]{2,1,0:T(8,128)(2,1)} %all-gather.3.cloned.1.call-done), channel_id=1, source_target_pairs={{0,1},{1,0},{2,3},{3,2},{4,5},{5,4},{6,7},{7,6},{8,9},{9,8},{10,11... | collective-permute-start | bytes 7077896 | tf_op jit(solution)/shard_map/ppermute | solution.py:101
  109.2 4.5 %copy-start.11 = (bf16[128,1024]{1,0:T(8,128)(2,1)S(1)}, bf16[128,1024]{1,0:T(8,128)(2,1)}, u32[]{:S(2)}) copy-start(bf16[128,1024]{1,0:T(8,128)(2,1)} %param.30) | copy-start | bytes 786436
  109.2 49.2 %all-to-all-start = ((bf16[8,24,4096]{2,1,0:T(8,128)(2,1)}), bf16[8,24,4096]{2,1,0:T(8,128)(2,1)S(1)}, u32[]{:S(2)}, u32[]{:S(2)}) async-start(bf16[8,24,4096]{2,1,0:T(8,128)(2,1)} %broadcast_in_dim.37), calls=%async_computation | async-start | bytes 3145728 | tf_op jit(solution)/shard_map/all_to_all | solution.py:123
  113.6 89.4 %all-gather.5.cloned.1.call-start = ((), (), s32[]{:S(2)}) async-start(), calls=%async_computation.4 | async-start | bytes 2949120 | tf_op jit(solution)/shard_map/all_gather | solution.py:149
  113.8 8.9 %collective-permute-start.12 = (bf16[1,160,512]{2,1,0:T(8,128)(2,1)S(1)}, bf16[1,160,512]{2,1,0:T(8,128)(2,1)S(1)}, u32[]{:S(2)}, u32[]{:S(2)}) collective-permute-start(bf16[1,160,512]{2,1,0:T(8,128)(2,1)S(1)} %maximum_bitcast_fusion), channel_id=1, source_target_pairs={{0,256},{32,288},{64,320},{96,352},{128,384},{160,416},{192,448},{... | collective-permute-start | bytes 491528 | tf_op jit(solution)/shard_map/ppermute | solution.py:106
  158.4 21.3 %collective-permute-start.7 = (bf16[192,4096]{1,0:T(8,128)(2,1)S(1)}, bf16[192,4096]{1,0:T(8,128)(2,1)S(1)}, u32[]{:S(2)}, u32[]{:S(2)}) collective-permute-start(bf16[192,4096]{1,0:T(8,128)(2,1)S(1)} %bitcast.166), channel_id=1, source_target_pairs={{0,1},{1,0},{2,3},{3,2},{4,5},{5,4},{6,7},{7,6},{8,9},{9,8},{10,11... | collective-permute-start | bytes 4718600 | tf_op jit(solution)/shard_map/ppermute | solution.py:101
  161.0 18.1 %collective-permute-start.6 = (bf16[4096,128]{1,0:T(8,128)(2,1)}, bf16[4096,128]{1,0:T(8,128)(2,1)S(1)}, u32[]{:S(2)}, u32[]{:S(2)}) collective-permute-start(bf16[4096,128]{1,0:T(8,128)(2,1)} %param.26), channel_id=1, source_target_pairs={{0,0},{1,256},{2,2},{3,258},{4,4},{5,260},{6,6},{7,262},{8,8},{9,2... | collective-permute-start | bytes 3145736 | tf_op jit(solution)/shard_map/ppermute | solution.py:119
  180.2 11.7 %copy-start.12 = (f32[2048]{0:T(1024)S(1)}, f32[2048]{0:T(1024)}, u32[]{:S(2)}) copy-start(f32[2048]{0:T(1024)} %param.27) | copy-start | bytes 24580
  181.3 18.5 %all-to-all-start.1 = ((bf16[8,2,192,128]{3,2,1,0:T(8,128)(2,1)}), bf16[8,2,192,128]{3,2,1,0:T(8,128)(2,1)S(1)}, u32[]{:S(2)}, u32[]{:S(2)}) async-start(bf16[8,2,192,128]{3,2,1,0:T(8,128)(2,1)} %broadcast_in_dim.38), calls=%async_computation.1 | async-start | bytes 1572864 | tf_op jit(solution)/shard_map/all_to_all | solution.py:123
  184.8 17.0 %collective-permute-start.9 = (bf16[3,2048,64]{1,2,0:T(8,128)(2,1)}, bf16[3,2048,64]{1,2,0:T(8,128)(2,1)S(1)}, u32[]{:S(2)}, u32[]{:S(2)}) collective-permute-start(bf16[3,2048,64]{1,2,0:T(8,128)(2,1)} %param.28), channel_id=1, source_target_pairs={{0,0},{1,256},{2,2},{3,258},{4,4},{5,260},{6,6},{7,262},{8,8},{9,2... | collective-permute-start | bytes 2359304 | tf_op jit(solution)/shard_map/ppermute | solution.py:119
  189.3 25.6 %collective-permute-start.10 = (bf16[64,2048]{1,0:T(8,128)(2,1)}, bf16[64,2048]{1,0:T(8,128)(2,1)}, u32[]{:S(2)}, u32[]{:S(2)}) collective-permute-start(bf16[64,2048]{1,0:T(8,128)(2,1)} %param.29), channel_id=1, source_target_pairs={{0,0},{1,256},{2,2},{3,258},{4,4},{5,260},{6,6},{7,262},{8,8},{9,2... | collective-permute-start | bytes 786440 | tf_op jit(solution)/shard_map/ppermute | solution.py:119
  199.9 8.3 %collective-permute-start.8 = (bf16[2,192,1024]{2,1,0:T(8,128)(2,1)S(1)}, bf16[2,192,1024]{2,1,0:T(8,128)(2,1)}, u32[]{:S(2)}, u32[]{:S(2)}) collective-permute-start(bf16[2,192,1024]{2,1,0:T(8,128)(2,1)S(1)} %copy_bitcast_fusion.1), channel_id=1, source_target_pairs={{0,1},{1,0},{2,3},{3,2},{4,5},{5,4},{6,7},{7,6},{8,9},{9,8},{10,11... | collective-permute-start | bytes 2359304 | tf_op jit(solution)/shard_map/ppermute | solution.py:101
  203.0 30.2 %collective-permute-start.13 = (bf16[2,1280,512]{2,1,0:T(8,128)(2,1)}, bf16[2,1280,512]{2,1,0:T(8,128)(2,1)}, u32[]{:S(2)}, u32[]{:S(2)}) collective-permute-start(bf16[2,1280,512]{2,1,0:T(8,128)(2,1)} %all-gather.5.cloned.1.call-done), channel_id=1, source_target_pairs={{0,1},{1,0},{2,3},{3,2},{4,5},{5,4},{6,7},{7,6},{8,9},{9,8},{10,11... | collective-permute-start | bytes 7864328 | tf_op jit(solution)/shard_map/ppermute | solution.py:101
  218.2 4.3 %collective-permute-start.11 = (bf16[192,2048]{1,0:T(8,128)(2,1)S(1)}, bf16[192,2048]{1,0:T(8,128)(2,1)}, u32[]{:S(2)}, u32[]{:S(2)}) collective-permute-start(bf16[192,2048]{1,0:T(8,128)(2,1)S(1)} %fusion.27), channel_id=1, source_target_pairs={{0,1},{1,0},{2,3},{3,2},{4,5},{5,4},{6,7},{7,6},{8,9},{9,8},{10,11... | collective-permute-start | bytes 2359304 | tf_op jit(solution)/shard_map/ppermute | solution.py:101
  225.2 25.3 %all-to-all-start.2 = ((bf16[8,24,2048]{2,1,0:T(8,128)(2,1)}), bf16[8,24,2048]{2,1,0:T(8,128)(2,1)S(1)}, u32[]{:S(2)}, u32[]{:S(2)}) async-start(bf16[8,24,2048]{2,1,0:T(8,128)(2,1)} %bitcast.170), calls=%async_computation.2 | async-start | bytes 1572864 | tf_op jit(solution)/shard_map/all_to_all | solution.py:123
  (12 other events, 21.7 us)
Sparse Core Ops, SparseCore 0:
  17.1 48.3 all-gather.2
  123.6 55.2 all-gather.4
